TPU v7x, 32 devices: a whole 2x2x4 slice. The times are simulated.
32 devices in a mesh: job: 2 (over y), dp: 1, expert: 16 (over z, x, core).
Axes of the slice: x: 2, y: 2, z: 4, core: 2. Of those that a mesh axis runs over, the one named last changes fastest.
Arguments:
- routes: int32 [512, 8], P(('job', 'dp', 'expert')), parts along dimension 0, may hold values from 0 to 15, all different within a row; in each aligned block of 16 rows (0 to 15, 16 to 31, ...) at most 12 rows name the same one
- gates: float32 [512, 8], P(('job', 'dp', 'expert')), parts along dimension 0, may hold values from 0.05 to 0.45
- grad_out: bfloat16 [512, 3584], P(('job', 'dp', 'expert')), parts along dimension 0, may hold values from -6 to 6
- hidden: bfloat16 [16, 2, 192, 1024], P('expert', ('job', 'dp')), parts along dimension 1, may hold values from -0.59765625 to 0.59765625
- down_weight: bfloat16 [16, 1024, 3584], P('expert', 'dp'), may hold values from -0.1875 to 0.1875
- adapter_a: bfloat16 [32, 16, 1024], P(('job', 'expert')), parts along dimension 0, may hold values from -1.5 to 1.5
- adapter_b: bfloat16 [32, 16, 3584], P(('job', 'expert')), parts along dimension 0, may hold values from -0.09375 to 0.09375
Outputs:
- grad_hidden: bfloat16 [16, 2, 192, 1024], P('expert', ('job', 'dp')), parts along dimension 1
- grad_gates: float32 [512, 8], P(('job', 'dp', 'expert')), parts along dimension 0
- grad_a: float32 [32, 16, 1024], P(('job', 'expert')), parts along dimension 0
- grad_b: float32 [32, 16, 3584], P(('job', 'expert')), parts along dimension 0
There are 2 independent parts, one for each index of `job`. A program takes and returns all parts, laid end to end along the dimension named above; an argument that names none is the same for every part. Nothing has to cross between parts.
Inputs may be any that keep to these rules, and one draw needn't show every extreme that they name: `routes`: each row names 8 different experts. Among the rows of one device no expert is named more than 12 times, a bound that some block reaches there in some devices.
All inputs are finite; a program needn't handle non-finite values.
Results may differ from a plain program's by a relative error of at most 0.015.
Values may be sent and summed in bfloat16 or wider, within the bound.
A program may use at most 64 MiB of HBM per device.

v0:
```python
import jax
import jax.numpy as jnp
from jax import lax
from jax.sharding import PartitionSpec as P

ADAPTER_SCALING = 1.0


def contract_product(left, right, left_dim, right_dim):
    return lax.dot_general(
        left, right, (((left_dim,), (right_dim,)), ((), ())), preferred_element_type=jnp.float32
    )


def expert_terms(
    frozen_gradient_term,
    grad_rows,
    gate_rows,
    hidden_slot_rows,
    adapter_down_factor,
    factor_b,
    gate_scaled_rows,
):
    lowrank_backward = contract_product(grad_rows, factor_b, 1, 1)
    passed_gradient = frozen_gradient_term + ADAPTER_SCALING * jnp.dot(
        lowrank_backward.astype(jnp.bfloat16),
        adapter_down_factor,
        preferred_element_type=jnp.float32,
    )
    grad_hid = (gate_rows[:, None] * passed_gradient).astype(jnp.bfloat16)
    slot_dgate = jnp.sum(hidden_slot_rows.astype(jnp.float32) * passed_gradient, axis=1)
    gate_weighted_output = (gate_rows[:, None] * lowrank_backward).astype(jnp.bfloat16)
    first_factor_term = ADAPTER_SCALING * contract_product(
        gate_weighted_output, hidden_slot_rows, 0, 0
    )
    lowrank_forward = contract_product(hidden_slot_rows, adapter_down_factor, 1, 1).astype(
        jnp.bfloat16
    )
    second_factor_term = ADAPTER_SCALING * contract_product(lowrank_forward, gate_scaled_rows, 0, 0)
    return (grad_hid, slot_dgate, first_factor_term, second_factor_term)


def shards(routes, gates, grad_out, hidden, down_weight, adapter_a, adapter_b):
    tok_rows, top_count = routes.shape
    experts = lax.axis_size("expert")
    slots = hidden.shape[2]
    capacity = slots // experts
    per_block = tok_rows * top_count
    chosen = routes.reshape(per_block)
    onehot = (chosen[:, None] == jnp.arange(experts, dtype=jnp.int32)[None, :]).astype(jnp.int32)
    position = jnp.sum((jnp.cumsum(onehot, axis=0) - onehot) * onehot, axis=1)
    slot_of = chosen * capacity + position
    placing = slot_of[:, None] == jnp.arange(slots, dtype=jnp.int32)[None, :]
    tok_place = jnp.any(placing.reshape(tok_rows, top_count, slots), axis=1).astype(jnp.bfloat16)
    send_grad = (
        contract_product(tok_place, grad_out, 0, 0)
        .astype(jnp.bfloat16)
        .reshape(experts, capacity, grad_out.shape[1])
    )
    send_gate = jnp.sum(jnp.where(placing, gates.reshape(per_block)[:, None], 0.0), axis=0).reshape(
        experts, capacity
    )
    recv_grad, recv_gate = (
        lax.all_to_all(send_grad, "expert", split_axis=0, concat_axis=0, tiled=True),
        lax.all_to_all(
            send_gate.astype(jnp.bfloat16), "expert", split_axis=0, concat_axis=0, tiled=True
        ).astype(send_gate.dtype),
    )
    grad_rows = recv_grad.reshape(slots, grad_out.shape[1])
    gate_rows = recv_gate.reshape(slots)
    hidden_slot_rows = hidden[0, 0]
    adapter_down_factor = adapter_a[0]
    factor_b = adapter_b[0]
    gate_scaled_rows = (gate_rows[:, None] * grad_rows.astype(jnp.float32)).astype(jnp.bfloat16)
    frozen_gradient_term = contract_product(
        grad_rows, lax.all_gather(down_weight[0], "dp", axis=0, tiled=True), 1, 1
    )
    grad_hid, slot_dgate, first_factor_term, second_factor_term = expert_terms(
        frozen_gradient_term,
        grad_rows,
        gate_rows,
        hidden_slot_rows,
        adapter_down_factor,
        factor_b,
        gate_scaled_rows,
    )
    gradient_first_factor, gradient_second_factor = (
        lax.psum(first_factor_term.astype(jnp.bfloat16), "dp").astype(jnp.float32),
        lax.psum(second_factor_term.astype(jnp.bfloat16), "dp").astype(jnp.float32),
    )
    back_gate = lax.all_to_all(
        slot_dgate.reshape(experts, capacity), "expert", split_axis=0, concat_axis=0, tiled=True
    )
    grad_gates = jnp.sum(
        jnp.where(placing, back_gate.reshape(slots)[None, :], 0.0), axis=1
    ).reshape(tok_rows, top_count)
    return (
        grad_hid[None, None],
        grad_gates,
        gradient_first_factor[None],
        gradient_second_factor[None],
    )


def solution(mesh):
    placed = (
        P(("job", "dp", "expert"), None),
        P(("job", "dp", "expert"), None),
        P(("job", "dp", "expert"), None),
        P("expert", ("job", "dp"), None, None),
        P("expert", "dp", None),
        P(("job", "expert"), None, None),
        P(("job", "expert"), None, None),
    )
    return jax.shard_map(
        shards,
        mesh=mesh,
        in_specs=placed,
        out_specs=(
            P("expert", ("job", "dp"), None, None),
            P(("job", "dp", "expert"), None),
            P(("job", "expert"), None, None),
            P(("job", "expert"), None, None),
        ),
        check_vma=False,
    )
```

profile of v0, /device:TPU:0, one launch (start us, length us, event | category | flops | bytes accessed | tf_op | source)
XLA Modules:
  0.0 88.3 jit_solution(11404284072833443136)
XLA Ops:
  0.6 0.8 copy.25
  1.6 0.2 reduce_window_sum.11
  1.8 0.2 select_reduce_fusion.2
  2.1 0.1 fusion.11
  2.2 0.6 convolution_convert_fusion
  2.8 0.4 reshape.68
  3.1 50.0 %all_to_all.20 = bf16[16,12,3584]{2,1,0:T(8,128)(2,1)} all-to-all(bf16[16,12,3584]{2,1,0:T(8,128)(2,1)S(1)} %reshape.68), channel_id=1, replica_groups=mesh['job'=2,'dp'=1,'expert'=16] {'expert'}, dimensions={0} | all-to-all | bytes 2752512 | tf_op jit(solution)/shard_map/all_to_all | solution.py:64
  53.2 2.4 %reshape.69 = bf16[192,3584]{1,0:T(8,128)(2,1)S(1)} reshape(bf16[16,12,3584]{2,1,0:T(8,128)(2,1)} %all_to_all.20) | data formatting | bytes 2752512 | tf_op jit(solution)/shard_map/reshape | solution.py:69
  55.6 0.4 fusion.12
  56.0 5.7 %fusion = f32[192,1024]{1,0:T(8,128)S(1)} fusion(bf16[192,3584]{1,0:T(8,128)(2,1)S(1)} %reshape.69, bf16[1,1024,3584]{2,1,0:T(8,128)(2,1)} %param.11), kind=kOutput, calls=%fused_computation | convolution fusion | flops 1409286144 | bytes 9502720 | tf_op jit(solution)/shard_map/dot_general | solution.py:10
  61.7 0.4 multiply_reduce_fusion
  62.1 0.7 all_to_all.15
  62.8 4.0 %all-to-all-start.2 = ((f32[16,1,12]{2,1,0:T(1,128)}), f32[16,1,12]{2,1,0:T(1,128)S(1)}, u32[]{:S(2)}, u32[]{:S(2)}) async-start(f32[16,1,12]{2,1,0:T(1,128)} %bitcast.5), calls=%async_computation.2 | async-start | bytes 16384 | tf_op jit(solution)/shard_map/all_to_all | solution.py:91
  67.0 6.1 %all-to-all-done.2 = f32[16,1,12]{2,1,0:T(1,128)S(1)} async-done(((f32[16,1,12]{2,1,0:T(1,128)}), f32[16,1,12]{2,1,0:T(1,128)S(1)}, u32[]{:S(2)}, u32[]{:S(2)}) %all-to-all-start.2) | async-done | bytes 800 | tf_op jit(solution)/shard_map/all_to_all | solution.py:91
  73.2 0.5 broadcast.21
  73.7 0.7 reduce.7
  74.5 0.2 select_reduce_fusion
  74.6 0.7 convert_element_type.75
  75.3 3.5 %all-to-all-start = ((bf16[16,1,12]{2,1,0:T(2,128)(2,1)}), bf16[16,1,12]{2,1,0:T(2,128)(2,1)S(1)}, u32[]{:S(2)}, u32[]{:S(2)}) async-start(bf16[16,1,12]{2,1,0:T(2,128)(2,1)} %convert_element_type.75), calls=%async_computation | async-start | bytes 16384 | tf_op jit(solution)/shard_map/all_to_all | solution.py:65
  78.9 0.7 copy.30
  79.6 5.5 %all-to-all-done = bf16[16,1,12]{2,1,0:T(2,128)(2,1)S(1)} async-done(((bf16[16,1,12]{2,1,0:T(2,128)(2,1)}), bf16[16,1,12]{2,1,0:T(2,128)(2,1)S(1)}, u32[]{:S(2)}, u32[]{:S(2)}) %all-to-all-start) | async-done | bytes 416 | tf_op jit(solution)/shard_map/all_to_all | solution.py:65
  85.2 0.8 fusion.6
  86.0 1.4 %fusion.3 = f32[1,16,3584]{2,1,0:T(8,128)} fusion(bf16[192,3584]{1,0:T(8,128)(2,1)S(1)} %reshape.69, f32[192]{0:T(256)S(1)} %reshape.71, bf16[1,1,192,1024]{3,2,1,0:T(8,128)(2,1)S(1)} %copy-done.1, bf16[1,16,1024]{2,1,0:T(8,128)(2,1)S(1)} %copy-done.2), kind=kOutput, calls=%fused_computation.5 | convolution fusion | flops 30493696 | bytes 2032384 | tf_op jit(solution)/shard_map/dot_general | solution.py:10
  87.4 0.9 fusion.7
  (21 shorter events, 0.7 us)
Async XLA Ops:
  0.6 1.6 %copy-start = (bf16[16,3584]{1,0:T(8,128)(2,1)S(1)}, bf16[16,3584]{1,0:T(8,128)(2,1)}, u32[]{:S(2)}) copy-start(bf16[16,3584]{1,0:T(8,128)(2,1)} %param.9) | copy-start | bytes 344068
  53.2 2.4 %copy-start.3 = (bf16[1,16,3584]{2,1,0:T(8,128)(2,1)S(1)}, bf16[1,16,3584]{2,1,0:T(8,128)(2,1)}, u32[]{:S(2)}) copy-start(bf16[1,16,3584]{2,1,0:T(8,128)(2,1)} %param.13) | copy-start | bytes 344068
  56.0 5.7 %copy-start.1 = (bf16[1,1,192,1024]{3,2,1,0:T(8,128)(2,1)S(1)}, bf16[1,1,192,1024]{3,2,1,0:T(8,128)(2,1)}, u32[]{:S(2)}) copy-start(bf16[1,1,192,1024]{3,2,1,0:T(8,128)(2,1)} %param.10) | copy-start | bytes 1179652
  56.0 5.7 %copy-start.2 = (bf16[1,16,1024]{2,1,0:T(8,128)(2,1)S(1)}, bf16[1,16,1024]{2,1,0:T(8,128)(2,1)}, u32[]{:S(2)}) copy-start(bf16[1,16,1024]{2,1,0:T(8,128)(2,1)} %param.12) | copy-start | bytes 98308
  61.7 5.1 %copy-start.4 = (f32[16,8]{0,1:T(8,128)S(1)}, f32[16,8]{0,1:T(8,128)}, u32[]{:S(2)}) copy-start(f32[16,8]{0,1:T(8,128)} %param.8) | copy-start | bytes 1540
  62.8 10.4 %all-to-all-start.2 = ((f32[16,1,12]{2,1,0:T(1,128)}), f32[16,1,12]{2,1,0:T(1,128)S(1)}, u32[]{:S(2)}, u32[]{:S(2)}) async-start(f32[16,1,12]{2,1,0:T(1,128)} %bitcast.5), calls=%async_computation.2 | async-start | bytes 16384 | tf_op jit(solution)/shard_map/all_to_all | solution.py:91
  75.3 9.8 %all-to-all-start = ((bf16[16,1,12]{2,1,0:T(2,128)(2,1)}), bf16[16,1,12]{2,1,0:T(2,128)(2,1)S(1)}, u32[]{:S(2)}, u32[]{:S(2)}) async-start(bf16[16,1,12]{2,1,0:T(2,128)(2,1)} %convert_element_type.75), calls=%async_computation | async-start | bytes 16384 | tf_op jit(solution)/shard_map/all_to_all | solution.py:65
where the time goes:
time: 88.6 us; the launch traced here: 88.3 us
  blocking collectives  50 us (56%)
  waiting for transfers between devices  11.7 us (13%)
  matrix products  9.24 us (10%)
  starting transfers between devices  7.49 us (8%)
  local copies, waits for them, and re-layouts  6.74 us (8%)
  other arithmetic  2.3 us (3%)
    all_to_all x1, blocking collectives, shards(): lax.all_to_all(send_grad, 'expert', split_axis=0, concat_axis=0, tiled=True)  50 us
    dot_general x5, matrix products, contract_product(): lax.dot_general(left, right, (((left_dim,), (right_dim,)), ((), ())), pre...  8.85 us
    all_to_all x1, waiting for transfers between devices, shards(): lax.all_to_all(slot_dgate.reshape(experts, capacity), 'expert', split_axi...  6.15 us
    all_to_all x1, waiting for transfers between devices, shards(): lax.all_to_all(send_gate.astype(jnp.bfloat16), 'expert', split_axis=0, co...  5.54 us
    all_to_all x1, starting transfers between devices, shards(): lax.all_to_all(slot_dgate.reshape(experts, capacity), 'expert', split_axi...  4.02 us
    all_to_all x1, starting transfers between devices, shards(): lax.all_to_all(send_gate.astype(jnp.bfloat16), 'expert', split_axis=0, co...  3.47 us
    reshape x1, local copies, waits for them, and re-layouts, shards(): grad_rows = recv_grad.reshape(slots, grad_out.shape[1])  2.4 us
  transfers between devices with their start and end apart: 2, of which 2 were waited for; matrix products, arithmetic and copies ran while one was open for 1% of the time, Pallas kernels for 0%

commit v1 on v0

--- a/solution.py
+++ b/solution.py
@@ -1,9 +1,14 @@
+import functools
+
 import jax
 import jax.numpy as jnp
 from jax import lax
+from jax.experimental import pallas as pl
+from jax.experimental.pallas import tpu as pltpu
 from jax.sharding import PartitionSpec as P
 
 ADAPTER_SCALING = 1.0
+MESH = pl.DeviceIdType.MESH
 
 
 def contract_product(left, right, left_dim, right_dim):
@@ -102,6 +107,286 @@
     )
 
 
+def flip(value, bit):
+    return value + bit - 2 * bit * ((value // bit) % 2)
+
+
+def xor(value, mask):
+    bit = 1
+    while bit <= mask:
+        if mask & bit:
+            value = flip(value, bit)
+        bit *= 2
+    return value
+
+
+def one_hot(shape, pick):
+    rows = lax.broadcasted_iota(jnp.int32, shape, 0)
+    columns = lax.broadcasted_iota(jnp.int32, shape, 1)
+    return pick(rows, columns).astype(jnp.bfloat16)
+
+
+def tile_of(size, most):
+    tile = most
+    while size % tile:
+        tile //= 2
+    return tile
+
+
+def fused_kernel(
+    experts,
+    routes_ref,
+    gates_ref,
+    grad_ref,
+    hidden_ref,
+    weight_hbm,
+    a_ref,
+    b_ref,
+    grad_hid_ref,
+    grad_gates_ref,
+    grad_a_ref,
+    grad_b_ref,
+    tokens,
+    weight,
+    rows,
+    products,
+    back_out,
+    back_in,
+    weight_sem,
+    send_sem,
+    recv_sem,
+    back_send_sem,
+    back_recv_sem,
+):
+    me = lax.axis_index("expert")
+    tok_rows, top_count = routes_ref.shape
+    features = grad_ref.shape[1]
+    slots, units = hidden_ref.shape
+    capacity = slots // experts
+    total = experts * tok_rows
+    planes = experts // 4
+    z, x, core = me // 4, (me // 2) % 2, me % 2
+    bf16, f32 = jnp.bfloat16, jnp.float32
+
+    load_weight = pltpu.make_async_copy(weight_hbm, weight, weight_sem)
+    load_weight.start()
+
+    barrier = pltpu.get_barrier_semaphore()
+    for step in range(1, experts):
+        pl.semaphore_signal(
+            barrier,
+            inc=1,
+            device_id={"expert": lax.rem(me + step, experts)},
+            device_id_type=MESH,
+        )
+
+    tokens[me, :, :features] = grad_ref[...]
+    high = gates_ref[...].astype(bf16)
+    low = (gates_ref[...] - high.astype(f32)).astype(bf16)
+    meta = jnp.zeros((tok_rows, 128), f32)
+    for part, values in enumerate((routes_ref[...].astype(f32).astype(bf16), high, low)):
+        spread = one_hot((top_count, 128), lambda r, c: c == r + part * top_count)
+        meta = meta + contract_product(values, spread, 1, 0)
+    tokens[me, :, features:] = meta.astype(bf16)
+    pl.semaphore_wait(barrier, experts - 1)
+
+    def index(plane, column, lane):
+        return plane * 4 + column * 2 + lane
+
+    x_mate, core_mate = index(z, 1 - x, core), index(z, x, 1 - core)
+    sent = []
+
+    def send(shard, target):
+        copy = pltpu.make_async_remote_copy(
+            src_ref=tokens.at[shard],
+            dst_ref=tokens.at[shard],
+            send_sem=send_sem.at[len(sent)],
+            recv_sem=recv_sem.at[shard],
+            device_id={"expert": target},
+            device_id_type=MESH,
+        )
+        copy.start()
+        sent.append(copy)
+
+    def arrived(shard):
+        pltpu.make_async_remote_copy(
+            src_ref=tokens.at[shard],
+            dst_ref=tokens.at[shard],
+            send_sem=send_sem.at[0],
+            recv_sem=recv_sem.at[shard],
+            device_id={"expert": core_mate},
+            device_id_type=MESH,
+        ).wait_recv()
+
+    send(me, x_mate)
+    for step in range(1, planes):
+        send(me, index(xor(z, step), x, core))
+    send(me, core_mate)
+    for step in range(planes):
+        plane = xor(z, step)
+        if step > 0:
+            mine = index(plane, x, core)
+            arrived(mine)
+            send(mine, x_mate)
+            send(mine, core_mate)
+        if step == planes - 1:
+            hidden = hidden_ref[...]
+            low_fwd = contract_product(hidden, a_ref[...], 1, 1)
+        if step > 0:
+            across = index(xor(z, step - 1), 1 - x, core)
+            arrived(across)
+            send(across, core_mate)
+    across = index(xor(z, planes - 1), 1 - x, core)
+    arrived(across)
+    send(across, core_mate)
+    for step in range(planes):
+        arrived(index(xor(z, step), x, 1 - core))
+        arrived(index(xor(z, step), 1 - x, 1 - core))
+
+    gathered = tokens[:, :, features:].reshape(total, 128)
+    eye = one_hot((128, 128), lambda r, c: r == c)
+    turned = contract_product(eye, gathered, 1, 1)
+    named = turned[:top_count] == me.astype(f32)
+    gate_of = jnp.where(
+        named, turned[top_count : 2 * top_count] + turned[2 * top_count : 3 * top_count], 0.0
+    )
+    gate_tok = jnp.sum(gate_of, axis=0, keepdims=True)
+    match = jnp.sum(named.astype(f32), axis=0, keepdims=True)
+    before = one_hot((total, total), lambda r, c: (r < c) & (r // tok_rows == c // tok_rows))
+    position = contract_product(
+        jnp.broadcast_to(match, (8, total)).astype(bf16), before, 1, 0
+    )[:1]
+    block = lax.broadcasted_iota(jnp.int32, (1, total), 1) // tok_rows
+    slot_of = jnp.where(match > 0.0, block.astype(f32) * capacity + position, -1.0)
+    slot_ids = lax.broadcasted_iota(jnp.int32, (slots, total), 0).astype(f32)
+    placing = slot_ids == slot_of
+    gate = jnp.sum(jnp.where(placing, gate_tok, 0.0), axis=1, keepdims=True)
+    place = placing.astype(bf16)
+
+    wide = tile_of(features, 512)
+
+    @pl.loop(0, features // wide)
+    def _(tile):
+        columns = pl.ds(pl.multiple_of(tile * wide, wide), wide)
+        rows[:, columns] = contract_product(
+            place, tokens[:, :, columns].reshape(total, wide), 1, 0
+        ).astype(bf16)
+
+    low_back = contract_product(rows[...], b_ref[...], 1, 1)
+    low_back_b = low_back.astype(bf16)
+    load_weight.wait()
+    deep = tile_of(units, 256)
+    products[...] = jnp.zeros_like(products)
+
+    @pl.loop(0, units // deep)
+    def _(tile):
+        span = pl.ds(pl.multiple_of(tile * deep, deep), deep)
+        through = contract_product(rows[...], weight[span, :], 1, 1)
+        through = through + contract_product(low_back_b, a_ref[:, span], 1, 0)
+        grad_hid_ref[:, span] = (gate * through).astype(bf16)
+        products[...] += hidden_ref[:, span].astype(f32) * through
+
+    dgate = jnp.sum(products[...], axis=1, keepdims=True)
+    dgate_tok = jnp.sum(jnp.where(placing, dgate, 0.0), axis=0, keepdims=True)
+    exact = lax.Precision.HIGHEST
+    source = lax.broadcasted_iota(jnp.int32, (experts, total), 0)
+    owner = lax.broadcasted_iota(jnp.int32, (experts, total), 1) // tok_rows
+    by_source = lax.dot_general(
+        jnp.where(source == owner, dgate_tok, 0.0),
+        one_hot((total, 128), lambda r, c: r % tok_rows == c).astype(f32),
+        (((1,), (0,)), ((), ())),
+        precision=exact,
+        preferred_element_type=f32,
+    )
+    back_out[...] = jnp.broadcast_to(by_source[:, None, :], back_out.shape)
+    returned = []
+    for step in range(1, experts):
+        target = lax.rem(me + step, experts)
+        copy = pltpu.make_async_remote_copy(
+            src_ref=back_out.at[target],
+            dst_ref=back_in.at[me],
+            send_sem=back_send_sem.at[step],
+            recv_sem=back_recv_sem.at[me],
+            device_id={"expert": target},
+            device_id_type=MESH,
+        )
+        copy.start()
+        returned.append(copy)
+    back_in[me] = back_out[me]
+
+    weighted = (gate * low_back).astype(bf16)
+    grad_a_ref[...] = contract_product(weighted, hidden_ref[...], 0, 0)
+    scaled = (gate * low_fwd).astype(bf16)
+
+    @pl.loop(0, features // wide)
+    def _(tile):
+        columns = pl.ds(pl.multiple_of(tile * wide, wide), wide)
+        grad_b_ref[:, columns] = contract_product(scaled, rows[:, columns], 0, 0)
+
+    for copy in sent:
+        copy.wait_send()
+    for copy in returned:
+        copy.wait_send()
+    for step in range(1, experts):
+        origin = lax.rem(me + step, experts)
+        pltpu.make_async_remote_copy(
+            src_ref=back_out.at[origin],
+            dst_ref=back_in.at[origin],
+            send_sem=back_send_sem.at[step],
+            recv_sem=back_recv_sem.at[origin],
+            device_id={"expert": origin},
+            device_id_type=MESH,
+        ).wait_recv()
+    back = lax.dot_general(
+        one_hot((tok_rows, 128), lambda r, c: r == c).astype(f32),
+        back_in[:, 0, :],
+        (((1,), (1,)), ((), ())),
+        precision=exact,
+        preferred_element_type=f32,
+    )
+    chosen = routes_ref[...]
+    picked = jnp.zeros((tok_rows, top_count), f32)
+    for expert in range(experts):
+        picked = picked + jnp.where(chosen == expert, back[:, expert : expert + 1], 0.0)
+    grad_gates_ref[...] = picked
+
+
+def fused_shards(experts, routes, gates, grad_out, hidden, down_weight, adapter_a, adapter_b):
+    tok_rows, top_count = routes.shape
+    features = grad_out.shape[1]
+    slots, units = hidden.shape[2:]
+    vmem = pl.BlockSpec(memory_space=pltpu.VMEM)
+    dma = pltpu.SemaphoreType.DMA
+    grad_hid, grad_gates, grad_a, grad_b = pl.pallas_call(
+        functools.partial(fused_kernel, experts),
+        out_shape=(
+            jax.ShapeDtypeStruct((slots, units), jnp.bfloat16),
+            jax.ShapeDtypeStruct((tok_rows, top_count), jnp.float32),
+            jax.ShapeDtypeStruct(adapter_a.shape[1:], jnp.float32),
+            jax.ShapeDtypeStruct(adapter_b.shape[1:], jnp.float32),
+        ),
+        in_specs=[vmem] * 4 + [pl.BlockSpec(memory_space=pl.ANY)] + [vmem] * 2,
+        out_specs=(vmem,) * 4,
+        scratch_shapes=[
+            pltpu.VMEM((experts, tok_rows, features + 128), jnp.bfloat16),
+            pltpu.VMEM((units, features), jnp.bfloat16),
+            pltpu.VMEM((slots, features), jnp.bfloat16),
+            pltpu.VMEM((slots, tile_of(units, 256)), jnp.float32),
+            pltpu.VMEM((experts, 8, 128), jnp.float32),
+            pltpu.VMEM((experts, 8, 128), jnp.float32),
+            dma,
+            dma((experts,)),
+            dma((experts,)),
+            dma((experts,)),
+            dma((experts,)),
+        ],
+        compiler_params=pltpu.CompilerParams(
+            collective_id=0, has_side_effects=True, vmem_limit_bytes=56 * 1024 * 1024
+        ),
+    )(routes, gates, grad_out, hidden[0, 0], down_weight[0], adapter_a[0], adapter_b[0])
+    return grad_hid[None, None], grad_gates, grad_a[None], grad_b[None]
+
+
 def solution(mesh):
     placed = (
         P(("job", "dp", "expert"), None),
@@ -112,8 +397,10 @@
         P(("job", "expert"), None, None),
         P(("job", "expert"), None, None),
     )
+    experts = mesh.shape["expert"]
+    fused = mesh.shape["dp"] == 1 and experts in (8, 16)
     return jax.shard_map(
-        shards,
+        functools.partial(fused_shards, experts) if fused else shards,
         mesh=mesh,
         in_specs=placed,
         out_specs=(

time: 88.6 us -> 44.3 us (0.50)
  blocking collectives: 50 us -> 0 us
  Pallas kernels: 0 us -> 34.4 us
  waiting for transfers between devices: 11.7 us -> 0 us
  matrix products: 9.24 us -> 0 us
  starting transfers between devices: 7.49 us -> 0 us
  other arithmetic: 2.3 us -> 0 us
  local copies, waits for them, and re-layouts: 6.74 us -> 8.95 us
    all_to_all x1 -> x0, blocking collectives: 50 us -> none  [shards(): lax.all_to_all(send_grad, 'expert', split_axis=0, concat_axis=0, tiled=True)]
    pallas_call x0 -> x1, Pallas kernels: none -> 34.4 us  [fused_shards(): pl.pallas_call(functools.partial(fused_kernel, experts), out_shape=(jax.S...]
    all_to_all x2 -> x0, waiting for transfers between devices: 11.7 us -> none  [the longest x1 6.15 us: shards(): lax.all_to_all(slot_dgate.reshape(experts, capacity), 'expert', split_axi...]
    dot_general x6 -> x0, matrix products: 9.24 us -> none  [the longest x5 8.85 us: contract_product(): lax.dot_general(left, right, (((left_dim,), (right_dim,)), ((), ())), pre...]
    all_to_all x2 -> x0, starting transfers between devices: 7.49 us -> none  [the longest x1 4.02 us: shards(): lax.all_to_all(slot_dgate.reshape(experts, capacity), 'expert', split_axi...]
    unnamed x13 -> x6, local copies, waits for them, and re-layouts: 1.57 us -> 8.95 us
    reshape x4 -> x0, local copies, waits for them, and re-layouts: 2.92 us -> none  [the longest x1 2.4 us: shards(): grad_rows = recv_grad.reshape(slots, grad_out.shape[1])]
    all_to_all x2 -> x0, local copies, waits for them, and re-layouts: 1.21 us -> none  [shards(): lax.all_to_all(slot_dgate.reshape(experts, capacity), 'expert', split_axi...]
  transfers between devices with their start and end apart: 2 -> 0, of which waited for: 2 -> 0; matrix products, arithmetic and copies ran while one was open for 1% -> 0% of each run, Pallas kernels for 0% -> 0%
where the time goes in v1:
time: 44.3 us; the launch traced here: 43.9 us
  Pallas kernels  34.4 us (78%)
  local copies, waits for them, and re-layouts  8.95 us (20%)
  between operations  0.64 us (1%)
    pallas_call x1, Pallas kernels, fused_shards(): pl.pallas_call(functools.partial(fused_kernel, experts), out_shape=(jax.S...  34.4 us
    unnamed x6, local copies, waits for them, and re-layouts  8.95 us

profile of v1, /device:TPU:0, one launch (start us, length us, event | category | flops | bytes accessed | tf_op | source)
XLA Modules:
  0.0 43.9 jit_solution(2241007192909787961)
XLA Ops:
  0.6 1.4 %copy.11.routes_ref = s32[16,8]{1,0:T(8,128)} copy(s32[16,8]{0,1:T(8,128)} %param.7) | data formatting | bytes 1024 | tf_op args[0]
  2.0 1.4 %copy.12.gates_ref = f32[16,8]{1,0:T(8,128)} copy(f32[16,8]{0,1:T(8,128)} %param.8) | data formatting | bytes 1024 | tf_op args[1]
  3.3 34.4 %shard_map.102 = (bf16[192,1024]{1,0:T(8,128)(2,1)}, f32[16,8]{1,0:T(8,128)}, f32[16,1024]{1,0:T(8,128)}, f32[16,3584]{1,0:T(8,128)}) custom-call(s32[16,8]{1,0:T(8,128)} %copy.11.routes_ref, f32[16,8]{1,0:T(8,128)} %copy.12.gates_ref, bf16[16,3584]{1,0:T(8,128)(2,1)} %grad_ref.1, bf16[192,1024]{1,0:T(8,128)(2,1)} %bitcast.8, bf16[1024,3584]{1,0:T(8,128)(2,1)} %bitcast.7, ...), custom_call_target="tpu_custom_call" | custom-call | tf_op jit(solution)/shard_map/pallas_call | solution.py:360
  37.7 1.4 %copy.13 = f32[16,8]{0,1:T(8,128)} copy(f32[16,8]{1,0:T(8,128)} %get-tuple-element.13) | data formatting | bytes 1024
  39.1 1.8 %copy.17 = bf16[1,1,192,1024]{3,2,1,0:T(8,128)(2,1)} copy(bf16[1,1,192,1024]{3,2,1,0:T(8,128)(2,1)} %bitcast.9) | data formatting | bytes 786432
  40.8 1.5 %copy.18 = f32[1,16,1024]{2,1,0:T(8,128)} copy(f32[1,16,1024]{2,1,0:T(8,128)} %bitcast.12) | data formatting | bytes 131072
  42.3 1.6 %copy.19 = f32[1,16,3584]{2,1,0:T(8,128)} copy(f32[1,16,3584]{2,1,0:T(8,128)} %bitcast.10) | data formatting | bytes 458752

commit v2 on v1

--- a/solution.py
+++ b/solution.py
@@ -9,6 +9,7 @@
 
 ADAPTER_SCALING = 1.0
 MESH = pl.DeviceIdType.MESH
+CHUNKS = 2
 
 
 def contract_product(left, right, left_dim, right_dim):
@@ -146,10 +147,12 @@
     grad_gates_ref,
     grad_a_ref,
     grad_b_ref,
+    meta_tokens,
     tokens,
     weight,
     rows,
-    products,
+    through_sum,
+    before,
     back_out,
     back_in,
     weight_sem,
@@ -159,8 +162,9 @@
     back_recv_sem,
 ):
     me = lax.axis_index("expert")
-    tok_rows, top_count = routes_ref.shape
-    features = grad_ref.shape[1]
+    top_count, tok_rows = routes_ref.shape
+    chunks = tokens.shape[0] + 1
+    chunk = tokens.shape[3]
     slots, units = hidden_ref.shape
     capacity = slots // experts
     total = experts * tok_rows
@@ -180,14 +184,19 @@
             device_id_type=MESH,
         )
 
-    tokens[me, :, :features] = grad_ref[...]
+    def held(part, shard):
+        return meta_tokens.at[shard] if part == 0 else tokens.at[part - 1, shard]
+
+    meta_tokens[me, :, :chunk] = grad_ref[:, :chunk]
+    for part in range(1, chunks):
+        tokens[part - 1, me] = grad_ref[:, part * chunk : (part + 1) * chunk]
     high = gates_ref[...].astype(bf16)
     low = (gates_ref[...] - high.astype(f32)).astype(bf16)
     meta = jnp.zeros((tok_rows, 128), f32)
     for part, values in enumerate((routes_ref[...].astype(f32).astype(bf16), high, low)):
         spread = one_hot((top_count, 128), lambda r, c: c == r + part * top_count)
-        meta = meta + contract_product(values, spread, 1, 0)
-    tokens[me, :, features:] = meta.astype(bf16)
+        meta = meta + contract_product(values, spread, 0, 0)
+    meta_tokens[me, :, chunk:] = meta.astype(bf16)
     pl.semaphore_wait(barrier, experts - 1)
 
     def index(plane, column, lane):
@@ -196,104 +205,143 @@
     x_mate, core_mate = index(z, 1 - x, core), index(z, x, 1 - core)
     sent = []
 
-    def send(shard, target):
+    def send(part, shard, target):
         copy = pltpu.make_async_remote_copy(
-            src_ref=tokens.at[shard],
-            dst_ref=tokens.at[shard],
+            src_ref=held(part, shard),
+            dst_ref=held(part, shard),
             send_sem=send_sem.at[len(sent)],
-            recv_sem=recv_sem.at[shard],
+            recv_sem=recv_sem.at[part, shard],
             device_id={"expert": target},
             device_id_type=MESH,
         )
         copy.start()
         sent.append(copy)
 
-    def arrived(shard):
+    def arrived(part, shard):
         pltpu.make_async_remote_copy(
-            src_ref=tokens.at[shard],
-            dst_ref=tokens.at[shard],
+            src_ref=held(part, shard),
+            dst_ref=held(part, shard),
             send_sem=send_sem.at[0],
-            recv_sem=recv_sem.at[shard],
+            recv_sem=recv_sem.at[part, shard],
             device_id={"expert": core_mate},
             device_id_type=MESH,
         ).wait_recv()
 
-    send(me, x_mate)
-    for step in range(1, planes):
-        send(me, index(xor(z, step), x, core))
-    send(me, core_mate)
-    for step in range(planes):
-        plane = xor(z, step)
-        if step > 0:
-            mine = index(plane, x, core)
-            arrived(mine)
-            send(mine, x_mate)
-            send(mine, core_mate)
-        if step == planes - 1:
-            hidden = hidden_ref[...]
-            low_fwd = contract_product(hidden, a_ref[...], 1, 1)
-        if step > 0:
-            across = index(xor(z, step - 1), 1 - x, core)
-            arrived(across)
-            send(across, core_mate)
-    across = index(xor(z, planes - 1), 1 - x, core)
-    arrived(across)
-    send(across, core_mate)
-    for step in range(planes):
-        arrived(index(xor(z, step), x, 1 - core))
-        arrived(index(xor(z, step), 1 - x, 1 - core))
-
-    gathered = tokens[:, :, features:].reshape(total, 128)
-    eye = one_hot((128, 128), lambda r, c: r == c)
-    turned = contract_product(eye, gathered, 1, 1)
-    named = turned[:top_count] == me.astype(f32)
-    gate_of = jnp.where(
-        named, turned[top_count : 2 * top_count] + turned[2 * top_count : 3 * top_count], 0.0
-    )
-    gate_tok = jnp.sum(gate_of, axis=0, keepdims=True)
-    match = jnp.sum(named.astype(f32), axis=0, keepdims=True)
-    before = one_hot((total, total), lambda r, c: (r < c) & (r // tok_rows == c // tok_rows))
-    position = contract_product(
-        jnp.broadcast_to(match, (8, total)).astype(bf16), before, 1, 0
-    )[:1]
-    block = lax.broadcasted_iota(jnp.int32, (1, total), 1) // tok_rows
-    slot_of = jnp.where(match > 0.0, block.astype(f32) * capacity + position, -1.0)
-    slot_ids = lax.broadcasted_iota(jnp.int32, (slots, total), 0).astype(f32)
-    placing = slot_ids == slot_of
-    gate = jnp.sum(jnp.where(placing, gate_tok, 0.0), axis=1, keepdims=True)
-    place = placing.astype(bf16)
-
-    wide = tile_of(features, 512)
-
-    @pl.loop(0, features // wide)
-    def _(tile):
-        columns = pl.ds(pl.multiple_of(tile * wide, wide), wide)
-        rows[:, columns] = contract_product(
-            place, tokens[:, :, columns].reshape(total, wide), 1, 0
+    for part in range(chunks):
+        send(part, me, x_mate)
+        for step in range(1, planes):
+            send(part, me, index(xor(z, step), x, core))
+        send(part, me, core_mate)
+
+    before[...] = one_hot(
+        (total, total), lambda r, c: (r < c) & (lax.div(r, tok_rows) == lax.div(c, tok_rows))
+    )
+    low_fwd = contract_product(hidden_ref[...], a_ref[...], 1, 1)
+    state = {}
+    deep = tile_of(units, 256)
+
+    def core_arrived(part):
+        for step in range(planes):
+            arrived(part, index(xor(z, step), x, 1 - core))
+            arrived(part, index(xor(z, step), 1 - x, 1 - core))
+
+    def route():
+        gathered = meta_tokens[:, :, chunk:].reshape(total, 128)
+        eye = one_hot((128, 128), lambda r, c: r == c)
+        turned = contract_product(eye, gathered, 1, 1)
+        named = turned[:top_count] == me.astype(f32)
+        gate_of = jnp.where(
+            named, turned[top_count : 2 * top_count] + turned[2 * top_count : 3 * top_count], 0.0
+        )
+        gate_tok = jnp.sum(gate_of, axis=0, keepdims=True)
+        match = jnp.sum(named.astype(f32), axis=0, keepdims=True)
+        position = contract_product(
+            jnp.broadcast_to(match, (8, total)).astype(bf16), before[...], 1, 0
+        )[:1]
+        block = lax.div(lax.broadcasted_iota(jnp.int32, (1, total), 1), tok_rows)
+        slot_of = jnp.where(match > 0.0, block.astype(f32) * capacity + position, -1.0)
+        slot_ids = lax.broadcasted_iota(jnp.int32, (slots, total), 0).astype(f32)
+        placing = slot_ids == slot_of
+        state["slot_of"] = slot_of
+        state["gate"] = jnp.sum(jnp.where(placing, gate_tok, 0.0), axis=1, keepdims=True)
+        state["place"] = placing.astype(bf16)
+
+    def columns(part):
+        return slice(part * chunk, (part + 1) * chunk)
+
+    def place_rows(part):
+        source = meta_tokens[:, :, :chunk] if part == 0 else tokens[part - 1]
+        rows[:, columns(part)] = contract_product(
+            state["place"], source.reshape(total, chunk), 1, 0
         ).astype(bf16)
-
-    low_back = contract_product(rows[...], b_ref[...], 1, 1)
+        low = contract_product(rows[:, columns(part)], b_ref[:, columns(part)], 1, 1)
+        state["low_back"] = low if part == 0 else state["low_back"] + low
+
+    def add_product(part, tile):
+        span = slice(tile * deep, (tile + 1) * deep)
+        product = contract_product(rows[:, columns(part)], weight[span, columns(part)], 1, 1)
+        if part == 0:
+            through_sum[:, span] = product
+        else:
+            through_sum[:, span] += product
+
+    def work_on(part):
+        def first():
+            core_arrived(part)
+            if part == 0:
+                route()
+                load_weight.wait()
+            place_rows(part)
+
+        return [first] + [
+            functools.partial(add_product, part, tile) for tile in range(units // deep)
+        ]
+
+    for part in range(chunks):
+        work = work_on(part - 1) if part > 0 else []
+        for step in range(planes):
+            if step > 0:
+                mine = index(xor(z, step), x, core)
+                arrived(part, mine)
+                send(part, mine, x_mate)
+                send(part, mine, core_mate)
+            across = index(xor(z, step), 1 - x, core)
+            if step < planes - 1:
+                arrived(part, across)
+                send(part, across, core_mate)
+            if work:
+                work.pop(0)()
+        while work:
+            work.pop(0)()
+        across = index(xor(z, planes - 1), 1 - x, core)
+        arrived(part, across)
+        send(part, across, core_mate)
+    last = chunks - 1
+    core_arrived(last)
+    place_rows(last)
+
+    gate, low_back = state["gate"], state["low_back"]
     low_back_b = low_back.astype(bf16)
-    load_weight.wait()
-    deep = tile_of(units, 256)
-    products[...] = jnp.zeros_like(products)
-
-    @pl.loop(0, units // deep)
-    def _(tile):
-        span = pl.ds(pl.multiple_of(tile * deep, deep), deep)
-        through = contract_product(rows[...], weight[span, :], 1, 1)
+    dgate = jnp.zeros((slots, 1), f32)
+    for tile in range(units // deep):
+        span = slice(tile * deep, (tile + 1) * deep)
+        through = through_sum[:, span] + contract_product(
+            rows[:, columns(last)], weight[span, columns(last)], 1, 1
+        )
         through = through + contract_product(low_back_b, a_ref[:, span], 1, 0)
         grad_hid_ref[:, span] = (gate * through).astype(bf16)
-        products[...] += hidden_ref[:, span].astype(f32) * through
-
-    dgate = jnp.sum(products[...], axis=1, keepdims=True)
-    dgate_tok = jnp.sum(jnp.where(placing, dgate, 0.0), axis=0, keepdims=True)
+        dgate = dgate + jnp.sum(hidden_ref[:, span].astype(f32) * through, axis=1, keepdims=True)
+
+    slot_ids = lax.broadcasted_iota(jnp.int32, (slots, total), 0).astype(f32)
+    dgate_tok = jnp.sum(
+        jnp.where(slot_ids == state["slot_of"], dgate, 0.0), axis=0, keepdims=True
+    )
     exact = lax.Precision.HIGHEST
     source = lax.broadcasted_iota(jnp.int32, (experts, total), 0)
-    owner = lax.broadcasted_iota(jnp.int32, (experts, total), 1) // tok_rows
+    owner = lax.div(lax.broadcasted_iota(jnp.int32, (experts, total), 1), tok_rows)
     by_source = lax.dot_general(
         jnp.where(source == owner, dgate_tok, 0.0),
-        one_hot((total, 128), lambda r, c: r % tok_rows == c).astype(f32),
+        one_hot((total, 128), lambda r, c: lax.rem(r, tok_rows) == c).astype(f32),
         (((1,), (0,)), ((), ())),
         precision=exact,
         preferred_element_type=f32,
@@ -317,11 +365,8 @@
     weighted = (gate * low_back).astype(bf16)
     grad_a_ref[...] = contract_product(weighted, hidden_ref[...], 0, 0)
     scaled = (gate * low_fwd).astype(bf16)
-
-    @pl.loop(0, features // wide)
-    def _(tile):
-        columns = pl.ds(pl.multiple_of(tile * wide, wide), wide)
-        grad_b_ref[:, columns] = contract_product(scaled, rows[:, columns], 0, 0)
+    for part in range(chunks):
+        grad_b_ref[:, columns(part)] = contract_product(scaled, rows[:, columns(part)], 0, 0)
 
     for copy in sent:
         copy.wait_send()
@@ -338,53 +383,81 @@
             device_id_type=MESH,
         ).wait_recv()
     back = lax.dot_general(
-        one_hot((tok_rows, 128), lambda r, c: r == c).astype(f32),
         back_in[:, 0, :],
-        (((1,), (1,)), ((), ())),
+        one_hot((128, tok_rows), lambda r, c: r == c).astype(f32),
+        (((1,), (0,)), ((), ())),
         precision=exact,
         preferred_element_type=f32,
     )
     chosen = routes_ref[...]
-    picked = jnp.zeros((tok_rows, top_count), f32)
+    picked = jnp.zeros((top_count, tok_rows), f32)
     for expert in range(experts):
-        picked = picked + jnp.where(chosen == expert, back[:, expert : expert + 1], 0.0)
+        picked = picked + jnp.where(chosen == expert, back[expert : expert + 1, :], 0.0)
     grad_gates_ref[...] = picked
+
+
+def copy_kernel(*refs):
+    count = (len(refs) - 1) // 2
+    sems = refs[-1]
+    copies = [
+        pltpu.make_async_copy(refs[i], refs[count + i], sems.at[i]) for i in range(count)
+    ]
+    for copy in copies:
+        copy.start()
+    for copy in copies:
+        copy.wait()
 
 
 def fused_shards(experts, routes, gates, grad_out, hidden, down_weight, adapter_a, adapter_b):
     tok_rows, top_count = routes.shape
     features = grad_out.shape[1]
     slots, units = hidden.shape[2:]
+    chunks = CHUNKS
+    while features % (chunks * 128):
+        chunks -= 1
+    chunk = features // chunks
     vmem = pl.BlockSpec(memory_space=pltpu.VMEM)
+    hbm = pl.BlockSpec(memory_space=pl.ANY)
     dma = pltpu.SemaphoreType.DMA
-    grad_hid, grad_gates, grad_a, grad_b = pl.pallas_call(
+    out_shape = (
+        jax.ShapeDtypeStruct((slots, units), jnp.bfloat16),
+        jax.ShapeDtypeStruct((top_count, tok_rows), jnp.float32),
+        jax.ShapeDtypeStruct(adapter_a.shape[1:], jnp.float32),
+        jax.ShapeDtypeStruct(adapter_b.shape[1:], jnp.float32),
+    )
+    results = pl.pallas_call(
         functools.partial(fused_kernel, experts),
-        out_shape=(
-            jax.ShapeDtypeStruct((slots, units), jnp.bfloat16),
-            jax.ShapeDtypeStruct((tok_rows, top_count), jnp.float32),
-            jax.ShapeDtypeStruct(adapter_a.shape[1:], jnp.float32),
-            jax.ShapeDtypeStruct(adapter_b.shape[1:], jnp.float32),
-        ),
-        in_specs=[vmem] * 4 + [pl.BlockSpec(memory_space=pl.ANY)] + [vmem] * 2,
+        out_shape=out_shape,
+        in_specs=[vmem] * 4 + [hbm] + [vmem] * 2,
         out_specs=(vmem,) * 4,
         scratch_shapes=[
-            pltpu.VMEM((experts, tok_rows, features + 128), jnp.bfloat16),
+            pltpu.VMEM((experts, tok_rows, chunk + 128), jnp.bfloat16),
+            pltpu.VMEM((chunks - 1, experts, tok_rows, chunk), jnp.bfloat16),
             pltpu.VMEM((units, features), jnp.bfloat16),
             pltpu.VMEM((slots, features), jnp.bfloat16),
-            pltpu.VMEM((slots, tile_of(units, 256)), jnp.float32),
+            pltpu.VMEM((slots, units), jnp.float32),
+            pltpu.VMEM((experts * tok_rows, experts * tok_rows), jnp.bfloat16),
             pltpu.VMEM((experts, 8, 128), jnp.float32),
             pltpu.VMEM((experts, 8, 128), jnp.float32),
             dma,
-            dma((experts,)),
-            dma((experts,)),
+            dma((chunks * (experts - 1),)),
+            dma((chunks, experts)),
             dma((experts,)),
             dma((experts,)),
         ],
         compiler_params=pltpu.CompilerParams(
             collective_id=0, has_side_effects=True, vmem_limit_bytes=56 * 1024 * 1024
         ),
-    )(routes, gates, grad_out, hidden[0, 0], down_weight[0], adapter_a[0], adapter_b[0])
-    return grad_hid[None, None], grad_gates, grad_a[None], grad_b[None]
+    )(routes.T, gates.T, grad_out, hidden[0, 0], down_weight[0], adapter_a[0], adapter_b[0])
+    grad_hid, grad_gates, grad_a, grad_b = pl.pallas_call(
+        copy_kernel,
+        out_shape=out_shape,
+        in_specs=[hbm] * 4,
+        out_specs=(hbm,) * 4,
+        scratch_shapes=[dma((4,))],
+        compiler_params=pltpu.CompilerParams(vmem_limit_bytes=60 * 1024 * 1024),
+    )(*results)
+    return grad_hid[None, None], grad_gates.T, grad_a[None], grad_b[None]
 
 
 def solution(mesh):

time: 44.3 us -> 64.3 us (1.45)
  Pallas kernels: 34.4 us -> 63.5 us
  local copies, waits for them, and re-layouts: 8.95 us -> 0 us
    pallas_call x1 -> x2, Pallas kernels: 34.4 us -> 63.5 us  [the longest x1 41.4 us: fused_shards(): pl.pallas_call(functools.partial(fused_kernel, experts), out_shape=out_sh...]
    unnamed x6 -> x0, local copies, waits for them, and re-layouts: 8.95 us -> none
where the time goes in v2:
time: 64.3 us; the launch traced here: 64.1 us
  Pallas kernels  63.5 us (99%)
    pallas_call x1, Pallas kernels, fused_shards(): pl.pallas_call(functools.partial(fused_kernel, experts), out_shape=out_sh...  41.4 us
    pallas_call x1, Pallas kernels, fused_shards(): pl.pallas_call(copy_kernel, out_shape=out_shape, in_specs=[hbm] * 4, out_...  22.1 us

profile of v2, /device:TPU:0, one launch (start us, length us, event | category | flops | bytes accessed | tf_op | source)
XLA Modules:
  0.0 64.1 jit_solution(94157637011790827)
XLA Ops:
  0.6 41.4 %shard_map.102 = (bf16[192,1024]{1,0:T(8,128)(2,1)}, f32[8,16]{1,0:T(8,128)}, f32[16,1024]{1,0:T(8,128)}, f32[16,3584]{1,0:T(8,128)}) custom-call(s32[8,16]{1,0:T(8,128)} %bitcast.14, f32[8,16]{1,0:T(8,128)} %bitcast.15, bf16[16,3584]{1,0:T(8,128)(2,1)} %grad_ref.1, bf16[192,1024]{1,0:T(8,128)(2,1)} %bitcast.11, bf16[1024,3584]{1,0:T(8,128)(2,1)} %bitcast.10, ...), custom_call_target="tpu_custom_call" | custom-call | tf_op jit(solution)/shard_map/pallas_call | solution.py:428
  42.0 22.1 %shard_map.103 = (bf16[192,1024]{1,0:T(8,128)(2,1)}, f32[8,16]{1,0:T(8,128)}, f32[16,1024]{1,0:T(8,128)}, f32[16,3584]{1,0:T(8,128)}) custom-call(bf16[192,1024]{1,0:T(8,128)(2,1)} %get-tuple-element.12.refs_0_, f32[8,16]{1,0:T(8,128)} %get-tuple-element.13.refs_1_, f32[16,1024]{1,0:T(8,128)} %get-tuple-element.14.refs_2_, f32[16,3584]{1,0:T(8,128)} %get-tuple-element.15.refs_3_), custom_call_target="tpu_custom_call" | custom-call | tf_op jit(solution)/shard_map/pallas_call | solution.py:452

commit v3 on v1

--- a/solution.py
+++ b/solution.py
@@ -149,7 +149,7 @@
     tokens,
     weight,
     rows,
-    products,
+    before,
     back_out,
     back_in,
     weight_sem,
@@ -159,7 +159,7 @@
     back_recv_sem,
 ):
     me = lax.axis_index("expert")
-    tok_rows, top_count = routes_ref.shape
+    top_count, tok_rows = routes_ref.shape
     features = grad_ref.shape[1]
     slots, units = hidden_ref.shape
     capacity = slots // experts
@@ -180,15 +180,23 @@
             device_id_type=MESH,
         )
 
-    tokens[me, :, :features] = grad_ref[...]
+    def place_of(plane, column, lane):
+        return (column * 2 + lane) * planes + plane
+
+    own = place_of(z, x, core)
+    tokens[own, :, :features] = grad_ref[...]
     high = gates_ref[...].astype(bf16)
     low = (gates_ref[...] - high.astype(f32)).astype(bf16)
     meta = jnp.zeros((tok_rows, 128), f32)
     for part, values in enumerate((routes_ref[...].astype(f32).astype(bf16), high, low)):
         spread = one_hot((top_count, 128), lambda r, c: c == r + part * top_count)
-        meta = meta + contract_product(values, spread, 1, 0)
-    tokens[me, :, features:] = meta.astype(bf16)
+        meta = meta + contract_product(values, spread, 0, 0)
+    tokens[own, :, features:] = meta.astype(bf16)
     pl.semaphore_wait(barrier, experts - 1)
+
+    def source_of(token):
+        stored = lax.div(token, tok_rows)
+        return lax.rem(stored, planes) * 4 + lax.div(stored, planes)
 
     def index(plane, column, lane):
         return plane * 4 + column * 2 + lane
@@ -196,52 +204,56 @@
     x_mate, core_mate = index(z, 1 - x, core), index(z, x, 1 - core)
     sent = []
 
-    def send(shard, target):
+    def held(first, count):
+        return tokens.at[pl.ds(first, count)]
+
+    def send(first, count, target):
         copy = pltpu.make_async_remote_copy(
-            src_ref=tokens.at[shard],
-            dst_ref=tokens.at[shard],
+            src_ref=held(first, count),
+            dst_ref=held(first, count),
             send_sem=send_sem.at[len(sent)],
-            recv_sem=recv_sem.at[shard],
+            recv_sem=recv_sem.at[first],
             device_id={"expert": target},
             device_id_type=MESH,
         )
         copy.start()
         sent.append(copy)
 
-    def arrived(shard):
+    def arrived(first, count):
         pltpu.make_async_remote_copy(
-            src_ref=tokens.at[shard],
-            dst_ref=tokens.at[shard],
+            src_ref=held(first, count),
+            dst_ref=held(first, count),
             send_sem=send_sem.at[0],
-            recv_sem=recv_sem.at[shard],
+            recv_sem=recv_sem.at[first],
             device_id={"expert": core_mate},
             device_id_type=MESH,
         ).wait_recv()
 
-    send(me, x_mate)
+    near, far = 2 * (z // 2), 2 * (1 - z // 2)
+    send(own, 1, x_mate)
     for step in range(1, planes):
-        send(me, index(xor(z, step), x, core))
-    send(me, core_mate)
-    for step in range(planes):
-        plane = xor(z, step)
-        if step > 0:
-            mine = index(plane, x, core)
-            arrived(mine)
-            send(mine, x_mate)
-            send(mine, core_mate)
-        if step == planes - 1:
-            hidden = hidden_ref[...]
-            low_fwd = contract_product(hidden, a_ref[...], 1, 1)
-        if step > 0:
-            across = index(xor(z, step - 1), 1 - x, core)
-            arrived(across)
-            send(across, core_mate)
-    across = index(xor(z, planes - 1), 1 - x, core)
-    arrived(across)
-    send(across, core_mate)
-    for step in range(planes):
-        arrived(index(xor(z, step), x, 1 - core))
-        arrived(index(xor(z, step), 1 - x, 1 - core))
+        send(own, 1, index(xor(z, step), x, core))
+
+    before[...] = one_hot(
+        (total, total), lambda r, c: (r < c) & (lax.div(r, tok_rows) == lax.div(c, tok_rows))
+    )
+    low_fwd = contract_product(hidden_ref[...], a_ref[...], 1, 1)
+    beside = place_of(xor(z, 1), x, core)
+    arrived(beside, 1)
+    send(beside, 1, x_mate)
+    send(place_of(near, x, core), 2, core_mate)
+    arrived(place_of(z, 1 - x, core), 1)
+    for step in (2, 3):
+        arrived(place_of(xor(z, step), x, core), 1)
+    send(place_of(far, x, core), 2, x_mate)
+    send(place_of(far, x, core), 2, core_mate)
+    arrived(place_of(xor(z, 1), 1 - x, core), 1)
+    send(place_of(near, 1 - x, core), 2, core_mate)
+    arrived(place_of(far, 1 - x, core), 2)
+    send(place_of(far, 1 - x, core), 2, core_mate)
+    for column in (x, 1 - x):
+        for pair in (near, far):
+            arrived(place_of(pair, column, 1 - core), 2)
 
     gathered = tokens[:, :, features:].reshape(total, 128)
     eye = one_hot((128, 128), lambda r, c: r == c)
@@ -252,11 +264,10 @@
     )
     gate_tok = jnp.sum(gate_of, axis=0, keepdims=True)
     match = jnp.sum(named.astype(f32), axis=0, keepdims=True)
-    before = one_hot((total, total), lambda r, c: (r < c) & (r // tok_rows == c // tok_rows))
     position = contract_product(
-        jnp.broadcast_to(match, (8, total)).astype(bf16), before, 1, 0
+        jnp.broadcast_to(match, (8, total)).astype(bf16), before[...], 1, 0
     )[:1]
-    block = lax.broadcasted_iota(jnp.int32, (1, total), 1) // tok_rows
+    block = source_of(lax.broadcasted_iota(jnp.int32, (1, total), 1))
     slot_of = jnp.where(match > 0.0, block.astype(f32) * capacity + position, -1.0)
     slot_ids = lax.broadcasted_iota(jnp.int32, (slots, total), 0).astype(f32)
     placing = slot_ids == slot_of
@@ -264,36 +275,30 @@
     place = placing.astype(bf16)
 
     wide = tile_of(features, 512)
-
-    @pl.loop(0, features // wide)
-    def _(tile):
-        columns = pl.ds(pl.multiple_of(tile * wide, wide), wide)
+    for start in range(0, features, wide):
+        columns = slice(start, start + wide)
         rows[:, columns] = contract_product(
             place, tokens[:, :, columns].reshape(total, wide), 1, 0
         ).astype(bf16)
-
     low_back = contract_product(rows[...], b_ref[...], 1, 1)
     low_back_b = low_back.astype(bf16)
     load_weight.wait()
     deep = tile_of(units, 256)
-    products[...] = jnp.zeros_like(products)
-
-    @pl.loop(0, units // deep)
-    def _(tile):
-        span = pl.ds(pl.multiple_of(tile * deep, deep), deep)
+    dgate = jnp.zeros((slots, 1), f32)
+    for start in range(0, units, deep):
+        span = slice(start, start + deep)
         through = contract_product(rows[...], weight[span, :], 1, 1)
         through = through + contract_product(low_back_b, a_ref[:, span], 1, 0)
         grad_hid_ref[:, span] = (gate * through).astype(bf16)
-        products[...] += hidden_ref[:, span].astype(f32) * through
-
-    dgate = jnp.sum(products[...], axis=1, keepdims=True)
+        dgate = dgate + jnp.sum(hidden_ref[:, span].astype(f32) * through, axis=1, keepdims=True)
+
     dgate_tok = jnp.sum(jnp.where(placing, dgate, 0.0), axis=0, keepdims=True)
     exact = lax.Precision.HIGHEST
     source = lax.broadcasted_iota(jnp.int32, (experts, total), 0)
-    owner = lax.broadcasted_iota(jnp.int32, (experts, total), 1) // tok_rows
+    owner = source_of(lax.broadcasted_iota(jnp.int32, (experts, total), 1))
     by_source = lax.dot_general(
         jnp.where(source == owner, dgate_tok, 0.0),
-        one_hot((total, 128), lambda r, c: r % tok_rows == c).astype(f32),
+        one_hot((total, 128), lambda r, c: lax.rem(r, tok_rows) == c).astype(f32),
         (((1,), (0,)), ((), ())),
         precision=exact,
         preferred_element_type=f32,
@@ -317,10 +322,8 @@
     weighted = (gate * low_back).astype(bf16)
     grad_a_ref[...] = contract_product(weighted, hidden_ref[...], 0, 0)
     scaled = (gate * low_fwd).astype(bf16)
-
-    @pl.loop(0, features // wide)
-    def _(tile):
-        columns = pl.ds(pl.multiple_of(tile * wide, wide), wide)
+    for start in range(0, features, wide):
+        columns = slice(start, start + wide)
         grad_b_ref[:, columns] = contract_product(scaled, rows[:, columns], 0, 0)
 
     for copy in sent:
@@ -338,17 +341,23 @@
             device_id_type=MESH,
         ).wait_recv()
     back = lax.dot_general(
-        one_hot((tok_rows, 128), lambda r, c: r == c).astype(f32),
         back_in[:, 0, :],
-        (((1,), (1,)), ((), ())),
+        one_hot((128, tok_rows), lambda r, c: r == c).astype(f32),
+        (((1,), (0,)), ((), ())),
         precision=exact,
         preferred_element_type=f32,
     )
     chosen = routes_ref[...]
-    picked = jnp.zeros((tok_rows, top_count), f32)
+    picked = jnp.zeros((top_count, tok_rows), f32)
     for expert in range(experts):
-        picked = picked + jnp.where(chosen == expert, back[:, expert : expert + 1], 0.0)
+        picked = picked + jnp.where(chosen == expert, back[expert : expert + 1, :], 0.0)
     grad_gates_ref[...] = picked
+
+
+def copy_kernel(*refs):
+    count = len(refs) // 2
+    for i in range(count):
+        refs[count + i][...] = refs[i][...]
 
 
 def fused_shards(experts, routes, gates, grad_out, hidden, down_weight, adapter_a, adapter_b):
@@ -356,22 +365,24 @@
     features = grad_out.shape[1]
     slots, units = hidden.shape[2:]
     vmem = pl.BlockSpec(memory_space=pltpu.VMEM)
+    hbm = pl.BlockSpec(memory_space=pl.ANY)
     dma = pltpu.SemaphoreType.DMA
-    grad_hid, grad_gates, grad_a, grad_b = pl.pallas_call(
+    out_shape = (
+        jax.ShapeDtypeStruct((slots, units), jnp.bfloat16),
+        jax.ShapeDtypeStruct((top_count, tok_rows), jnp.float32),
+        jax.ShapeDtypeStruct(adapter_a.shape[1:], jnp.float32),
+        jax.ShapeDtypeStruct(adapter_b.shape[1:], jnp.float32),
+    )
+    results = pl.pallas_call(
         functools.partial(fused_kernel, experts),
-        out_shape=(
-            jax.ShapeDtypeStruct((slots, units), jnp.bfloat16),
-            jax.ShapeDtypeStruct((tok_rows, top_count), jnp.float32),
-            jax.ShapeDtypeStruct(adapter_a.shape[1:], jnp.float32),
-            jax.ShapeDtypeStruct(adapter_b.shape[1:], jnp.float32),
-        ),
-        in_specs=[vmem] * 4 + [pl.BlockSpec(memory_space=pl.ANY)] + [vmem] * 2,
+        out_shape=out_shape,
+        in_specs=[vmem] * 4 + [hbm] + [vmem] * 2,
         out_specs=(vmem,) * 4,
         scratch_shapes=[
             pltpu.VMEM((experts, tok_rows, features + 128), jnp.bfloat16),
             pltpu.VMEM((units, features), jnp.bfloat16),
             pltpu.VMEM((slots, features), jnp.bfloat16),
-            pltpu.VMEM((slots, tile_of(units, 256)), jnp.float32),
+            pltpu.VMEM((experts * tok_rows, experts * tok_rows), jnp.bfloat16),
             pltpu.VMEM((experts, 8, 128), jnp.float32),
             pltpu.VMEM((experts, 8, 128), jnp.float32),
             dma,
@@ -383,8 +394,15 @@
         compiler_params=pltpu.CompilerParams(
             collective_id=0, has_side_effects=True, vmem_limit_bytes=56 * 1024 * 1024
         ),
-    )(routes, gates, grad_out, hidden[0, 0], down_weight[0], adapter_a[0], adapter_b[0])
-    return grad_hid[None, None], grad_gates, grad_a[None], grad_b[None]
+    )(routes.T, gates.T, grad_out, hidden[0, 0], down_weight[0], adapter_a[0], adapter_b[0])
+    grad_hid, grad_gates, grad_a, grad_b = pl.pallas_call(
+        copy_kernel,
+        out_shape=out_shape,
+        in_specs=[vmem] * 4,
+        out_specs=(vmem,) * 4,
+        compiler_params=pltpu.CompilerParams(vmem_limit_bytes=60 * 1024 * 1024),
+    )(*results)
+    return grad_hid[None, None], grad_gates.T, grad_a[None], grad_b[None]
 
 
 def solution(mesh):
@@ -398,7 +416,7 @@
         P(("job", "expert"), None, None),
     )
     experts = mesh.shape["expert"]
-    fused = mesh.shape["dp"] == 1 and experts in (8, 16)
+    fused = mesh.shape["dp"] == 1 and experts == 16
     return jax.shard_map(
         functools.partial(fused_shards, experts) if fused else shards,
         mesh=mesh,

time: 44.3 us -> 38.4 us (0.87)
  local copies, waits for them, and re-layouts: 8.95 us -> 0 us
  Pallas kernels: 34.4 us -> 37.6 us
    unnamed x6 -> x0, local copies, waits for them, and re-layouts: 8.95 us -> none
    pallas_call x1 -> x2, Pallas kernels: 34.4 us -> 37.6 us  [the longest x1 35.6 us: fused_shards(): pl.pallas_call(functools.partial(fused_kernel, experts), out_shape=out_sh...]
where the time goes in v3:
time: 38.4 us; the launch traced here: 38.2 us
  Pallas kernels  37.6 us (98%)
  between operations  0.64 us (2%)
    pallas_call x1, Pallas kernels, fused_shards(): pl.pallas_call(functools.partial(fused_kernel, experts), out_shape=out_sh...  35.6 us
    pallas_call x1, Pallas kernels, fused_shards(): pl.pallas_call(copy_kernel, out_shape=out_shape, in_specs=[vmem] * 4, out...  1.96 us

profile of v3, /device:TPU:0, one launch (start us, length us, event | category | flops | bytes accessed | tf_op | source)
XLA Modules:
  0.0 38.2 jit_solution(12133637855179829074)
XLA Ops:
  0.6 35.6 %shard_map.102 = (bf16[192,1024]{1,0:T(8,128)(2,1)}, f32[8,16]{1,0:T(8,128)}, f32[16,1024]{1,0:T(8,128)}, f32[16,3584]{1,0:T(8,128)}) custom-call(s32[8,16]{1,0:T(8,128)} %bitcast.14, f32[8,16]{1,0:T(8,128)} %bitcast.15, bf16[16,3584]{1,0:T(8,128)(2,1)} %grad_ref.1, bf16[192,1024]{1,0:T(8,128)(2,1)} %bitcast.11, bf16[1024,3584]{1,0:T(8,128)(2,1)} %bitcast.10, ...), custom_call_target="tpu_custom_call" | custom-call | tf_op jit(solution)/shard_map/pallas_call | solution.py:376
  36.2 2.0 %shard_map.103 = (bf16[192,1024]{1,0:T(8,128)(2,1)}, f32[8,16]{1,0:T(8,128)}, f32[16,1024]{1,0:T(8,128)}, f32[16,3584]{1,0:T(8,128)}) custom-call(bf16[192,1024]{1,0:T(8,128)(2,1)} %get-tuple-element.12.refs_0_, f32[8,16]{1,0:T(8,128)} %get-tuple-element.13.refs_1_, f32[16,1024]{1,0:T(8,128)} %get-tuple-element.14.refs_2_, f32[16,3584]{1,0:T(8,128)} %get-tuple-element.15.refs_3_), custom_call_target="tpu_custom_call" | custom-call | tf_op jit(solution)/shard_map/pallas_call | solution.py:398

commit v4 on v3

--- a/solution.py
+++ b/solution.py
@@ -244,12 +244,14 @@
     send(place_of(near, x, core), 2, core_mate)
     arrived(place_of(z, 1 - x, core), 1)
     for step in (2, 3):
-        arrived(place_of(xor(z, step), x, core), 1)
-    send(place_of(far, x, core), 2, x_mate)
+        distant = place_of(xor(z, step), x, core)
+        arrived(distant, 1)
+        send(distant, 1, x_mate)
     send(place_of(far, x, core), 2, core_mate)
     arrived(place_of(xor(z, 1), 1 - x, core), 1)
     send(place_of(near, 1 - x, core), 2, core_mate)
-    arrived(place_of(far, 1 - x, core), 2)
+    for step in (2, 3):
+        arrived(place_of(xor(z, step), 1 - x, core), 1)
     send(place_of(far, 1 - x, core), 2, core_mate)
     for column in (x, 1 - x):
         for pair in (near, far):

time: 38.4 us -> 35.9 us (0.935)
  Pallas kernels: 37.6 us -> 35.1 us
    pallas_call x1, Pallas kernels: 35.6 us -> 33.1 us  [fused_shards(): pl.pallas_call(functools.partial(fused_kernel, experts), out_shape=out_sh...]
where the time goes in v4:
time: 35.9 us; the launch traced here: 35.7 us
  Pallas kernels  35.1 us (98%)
  between operations  0.64 us (2%)
    pallas_call x1, Pallas kernels, fused_shards(): pl.pallas_call(functools.partial(fused_kernel, experts), out_shape=out_sh...  33.1 us
    pallas_call x1, Pallas kernels, fused_shards(): pl.pallas_call(copy_kernel, out_shape=out_shape, in_specs=[vmem] * 4, out...  1.96 us

profile of v4, /device:TPU:0, one launch (start us, length us, event | category | flops | bytes accessed | tf_op | source)
XLA Modules:
  0.0 35.7 jit_solution(18234435767484992877)
XLA Ops:
  0.6 33.1 %shard_map.102 = (bf16[192,1024]{1,0:T(8,128)(2,1)}, f32[8,16]{1,0:T(8,128)}, f32[16,1024]{1,0:T(8,128)}, f32[16,3584]{1,0:T(8,128)}) custom-call(s32[8,16]{1,0:T(8,128)} %bitcast.14, f32[8,16]{1,0:T(8,128)} %bitcast.15, bf16[16,3584]{1,0:T(8,128)(2,1)} %grad_ref.1, bf16[192,1024]{1,0:T(8,128)(2,1)} %bitcast.11, bf16[1024,3584]{1,0:T(8,128)(2,1)} %bitcast.10, ...), custom_call_target="tpu_custom_call" | custom-call | tf_op jit(solution)/shard_map/pallas_call | solution.py:378
  33.7 2.0 %shard_map.103 = (bf16[192,1024]{1,0:T(8,128)(2,1)}, f32[8,16]{1,0:T(8,128)}, f32[16,1024]{1,0:T(8,128)}, f32[16,3584]{1,0:T(8,128)}) custom-call(bf16[192,1024]{1,0:T(8,128)(2,1)} %get-tuple-element.12.refs_0_, f32[8,16]{1,0:T(8,128)} %get-tuple-element.13.refs_1_, f32[16,1024]{1,0:T(8,128)} %get-tuple-element.14.refs_2_, f32[16,3584]{1,0:T(8,128)} %get-tuple-element.15.refs_3_), custom_call_target="tpu_custom_call" | custom-call | tf_op jit(solution)/shard_map/pallas_call | solution.py:400

commit v5 on v4

--- a/solution.py
+++ b/solution.py
@@ -230,24 +230,52 @@
         ).wait_recv()
 
     near, far = 2 * (z // 2), 2 * (1 - z // 2)
+    inner = (z + 1) // 2 == 1
+    z_mate, middle_mate = index(xor(z, 1), x, core), index(xor(z, 3), x, core)
+    beside = place_of(xor(z, 1), x, core)
+    far_inner, far_outer = 2 - z // 2, 3 * (1 - z // 2)
+    hops = [
+        (own, middle_mate),
+        (beside, middle_mate),
+        (place_of(far_inner, x, core), z_mate),
+        (place_of(far_outer, x, core), z_mate),
+    ]
+
+    def hop(number):
+        shard, target = hops[number]
+        return pltpu.make_async_remote_copy(
+            src_ref=held(shard, 1),
+            dst_ref=held(shard, 1),
+            send_sem=send_sem.at[experts - 1 - number],
+            recv_sem=recv_sem.at[shard],
+            device_id={"expert": target},
+            device_id_type=MESH,
+        )
+
+    def pass_on(number):
+        @pl.when(inner)
+        def _():
+            hop(number).start()
+
+    send(own, 1, z_mate)
+    pass_on(0)
     send(own, 1, x_mate)
-    for step in range(1, planes):
-        send(own, 1, index(xor(z, step), x, core))
 
     before[...] = one_hot(
         (total, total), lambda r, c: (r < c) & (lax.div(r, tok_rows) == lax.div(c, tok_rows))
     )
     low_fwd = contract_product(hidden_ref[...], a_ref[...], 1, 1)
-    beside = place_of(xor(z, 1), x, core)
     arrived(beside, 1)
+    pass_on(1)
     send(beside, 1, x_mate)
     send(place_of(near, x, core), 2, core_mate)
-    arrived(place_of(z, 1 - x, core), 1)
-    for step in (2, 3):
-        distant = place_of(xor(z, step), x, core)
+    for number, plane in ((2, far_inner), (3, far_outer)):
+        distant = place_of(plane, x, core)
         arrived(distant, 1)
+        pass_on(number)
         send(distant, 1, x_mate)
     send(place_of(far, x, core), 2, core_mate)
+    arrived(place_of(z, 1 - x, core), 1)
     arrived(place_of(xor(z, 1), 1 - x, core), 1)
     send(place_of(near, 1 - x, core), 2, core_mate)
     for step in (2, 3):
@@ -330,6 +358,12 @@
 
     for copy in sent:
         copy.wait_send()
+
+    @pl.when(inner)
+    def _():
+        for number in range(len(hops)):
+            hop(number).wait_send()
+
     for copy in returned:
         copy.wait_send()
     for step in range(1, experts):

time: 35.9 us -> 36.7 us (1.022)
  Pallas kernels: 35.1 us -> 35.9 us
    pallas_call x1, Pallas kernels: 33.1 us -> 33.9 us  [fused_shards(): pl.pallas_call(functools.partial(fused_kernel, experts), out_shape=out_sh...]
where the time goes in v5:
time: 36.7 us; the launch traced here: 36.5 us
  Pallas kernels  35.9 us (98%)
  between operations  0.64 us (2%)
    pallas_call x1, Pallas kernels, fused_shards(): pl.pallas_call(functools.partial(fused_kernel, experts), out_shape=out_sh...  33.9 us
    pallas_call x1, Pallas kernels, fused_shards(): pl.pallas_call(copy_kernel, out_shape=out_shape, in_specs=[vmem] * 4, out...  1.96 us

profile of v5, /device:TPU:0, one launch (start us, length us, event | category | flops | bytes accessed | tf_op | source)
XLA Modules:
  0.0 36.5 jit_solution(8020690175749782815)
XLA Ops:
  0.6 33.9 %shard_map.102 = (bf16[192,1024]{1,0:T(8,128)(2,1)}, f32[8,16]{1,0:T(8,128)}, f32[16,1024]{1,0:T(8,128)}, f32[16,3584]{1,0:T(8,128)}) custom-call(s32[8,16]{1,0:T(8,128)} %bitcast.14, f32[8,16]{1,0:T(8,128)} %bitcast.15, bf16[16,3584]{1,0:T(8,128)(2,1)} %grad_ref.1, bf16[192,1024]{1,0:T(8,128)(2,1)} %bitcast.11, bf16[1024,3584]{1,0:T(8,128)(2,1)} %bitcast.10, ...), custom_call_target="tpu_custom_call" | custom-call | tf_op jit(solution)/shard_map/pallas_call | solution.py:412
  34.6 2.0 %shard_map.103 = (bf16[192,1024]{1,0:T(8,128)(2,1)}, f32[8,16]{1,0:T(8,128)}, f32[16,1024]{1,0:T(8,128)}, f32[16,3584]{1,0:T(8,128)}) custom-call(bf16[192,1024]{1,0:T(8,128)(2,1)} %get-tuple-element.12.refs_0_, f32[8,16]{1,0:T(8,128)} %get-tuple-element.13.refs_1_, f32[16,1024]{1,0:T(8,128)} %get-tuple-element.14.refs_2_, f32[16,3584]{1,0:T(8,128)} %get-tuple-element.15.refs_3_), custom_call_target="tpu_custom_call" | custom-call | tf_op jit(solution)/shard_map/pallas_call | solution.py:434

commit v6 on v4

--- a/solution.py
+++ b/solution.py
@@ -230,8 +230,9 @@
         ).wait_recv()
 
     near, far = 2 * (z // 2), 2 * (1 - z // 2)
+    send(own, 1, index(xor(z, 2), x, core))
     send(own, 1, x_mate)
-    for step in range(1, planes):
+    for step in (1, 3):
         send(own, 1, index(xor(z, step), x, core))
 
     before[...] = one_hot(

time: 35.9 us -> 36 us (level)
  no operation moved by 1% of the time
where the time goes in v6:
time: 36 us; the launch traced here: 35.8 us
  Pallas kernels  35.2 us (98%)
  between operations  0.64 us (2%)
    pallas_call x1, Pallas kernels, fused_shards(): pl.pallas_call(functools.partial(fused_kernel, experts), out_shape=out_sh...  33.2 us
    pallas_call x1, Pallas kernels, fused_shards(): pl.pallas_call(copy_kernel, out_shape=out_shape, in_specs=[vmem] * 4, out...  1.96 us

profile of v6, /device:TPU:0, one launch (start us, length us, event | category | flops | bytes accessed | tf_op | source)
XLA Modules:
  0.0 35.8 jit_solution(14928149306145677806)
XLA Ops:
  0.6 33.2 %shard_map.102 = (bf16[192,1024]{1,0:T(8,128)(2,1)}, f32[8,16]{1,0:T(8,128)}, f32[16,1024]{1,0:T(8,128)}, f32[16,3584]{1,0:T(8,128)}) custom-call(s32[8,16]{1,0:T(8,128)} %bitcast.14, f32[8,16]{1,0:T(8,128)} %bitcast.15, bf16[16,3584]{1,0:T(8,128)(2,1)} %grad_ref.1, bf16[192,1024]{1,0:T(8,128)(2,1)} %bitcast.11, bf16[1024,3584]{1,0:T(8,128)(2,1)} %bitcast.10, ...), custom_call_target="tpu_custom_call" | custom-call | tf_op jit(solution)/shard_map/pallas_call | solution.py:379
  33.9 2.0 %shard_map.103 = (bf16[192,1024]{1,0:T(8,128)(2,1)}, f32[8,16]{1,0:T(8,128)}, f32[16,1024]{1,0:T(8,128)}, f32[16,3584]{1,0:T(8,128)}) custom-call(bf16[192,1024]{1,0:T(8,128)(2,1)} %get-tuple-element.12.refs_0_, f32[8,16]{1,0:T(8,128)} %get-tuple-element.13.refs_1_, f32[16,1024]{1,0:T(8,128)} %get-tuple-element.14.refs_2_, f32[16,3584]{1,0:T(8,128)} %get-tuple-element.15.refs_3_), custom_call_target="tpu_custom_call" | custom-call | tf_op jit(solution)/shard_map/pallas_call | solution.py:401
